TPU v7x, 512 devices: a whole 4x4x16 slice. The times are simulated.
512 devices in a mesh: grp: 16 (over z), dom: 32 (over y, x, core).
Axes of the slice: x: 4, y: 4, z: 16, core: 2. Of those that a mesh axis runs over, the one named last changes fastest.
Arguments:
- state: float32 [6, 125, 131072], P(None, None, ('grp', 'dom')), may hold values from -0.6 to 0.6
- adjoint: float32 [6, 125, 131072], P(None, None, ('grp', 'dom')), may hold values from -16 to 16
- factors: float32 [3, 5, 5, 131072], P(None, None, None, ('grp', 'dom')), may hold values from -3 to 3
- order: int32 [131072], P(('grp', 'dom')), may hold values from 1 to 4
- marks: int32 [131072], P(('grp', 'dom')), may hold values from -1 to 1
- neighbours: int32 [6, 131072], P(None, ('grp', 'dom')), may hold values from 0 to 255
- new_owner: int32 [131072, 1], P(('grp', 'dom')), may hold values from 0 to 15; in each aligned block of 256 rows (0 to 255, 256 to 511, ...) at most 24 rows name the same one
Outputs:
- share: float32 [131072], P(('grp', 'dom'))
- moved_state: float32 [6, 125, 196608], P(None, None, ('grp', 'dom'))
- moved_adjoint: float32 [6, 125, 196608], P(None, None, ('grp', 'dom'))
- moved_factors: float32 [3, 5, 5, 196608], P(None, None, None, ('grp', 'dom'))
- moved_order: int32 [196608], P(('grp', 'dom'))
Inputs may be any that keep to these rules, and one draw needn't show every extreme that they name: `new_owner`: within each partition's 256 elements, no group index is named more than 24 times, and in every draw some group is named exactly 24 times by some partition.
All inputs are finite; a program needn't handle non-finite values.
Results may differ from a plain program's by a relative error of at most 0.0003.
Values sent between devices are 32-bit elements; how exact they have to be, the bound alone decides.
A program may use at most 128 MiB of HBM per device.

v0:
```python
import functools
import math

import jax
import jax.numpy as jnp
import ml_dtypes
import numpy as np
from jax import lax
from jax.experimental import pallas as pl
from jax.experimental.pallas import tpu as pltpu
from jax.sharding import PartitionSpec as P

NV = 6
PMAX = 4
P1 = 5
MODES = 125
NQ1 = 7
ELEM = 256
CAP = 24
GRP = 16
DOM = 32
SLOTS = GRP * CAP
LEAF = 8
ROWS = DOM // LEAF
MPAD = 128
PT = 56
TM = 32
KCAT = 3 * MPAD
FROWS = 3 * P1 * P1 + 1
SPARE = MPAD - MODES
REST = FROWS - 2 * NV * SPARE
REST_AT = 2 * NV * SPARE % 8
MESH = pl.DeviceIdType.MESH
CHUNKS = ((0, 1), (1, 3), (4, 4), (8, 4))
F32 = jnp.float32
BF16 = jnp.bfloat16


def line_tables():
    place = math.pi * (np.arange(NQ1) + 0.5) / NQ1
    points = -np.cos(place)
    weights = math.pi / NQ1 * np.sin(place)
    values = [np.ones(NQ1), points]
    slopes = [np.zeros(NQ1), np.ones(NQ1)]
    for n in range(1, P1 - 1):
        values.append(((2 * n + 1) * points * values[n] - n * values[n - 1]) / (n + 1))
        slopes.append(slopes[n - 1] + (2 * n + 1) * values[n])
    norm = np.sqrt((2 * np.arange(P1) + 1) / 2.0)
    vt = np.stack(values, axis=1) * norm
    st = np.stack(slopes, axis=1) * norm
    ends = [norm * (-1.0) ** np.arange(P1), norm]
    return vt, st, ends, weights


def split(table):
    high = table.astype(np.float32).astype(ml_dtypes.bfloat16)
    low = (table - high.astype(np.float64)).astype(np.float32).astype(ml_dtypes.bfloat16)
    return high, low


def against_split(table):
    rows, depth = table.shape
    pad = MPAD if depth == MODES else TM
    high, low = split(table)
    out = np.zeros((rows, 3 * pad), ml_dtypes.bfloat16)
    out[:, :depth] = high
    out[:, pad : pad + depth] = high
    out[:, 2 * pad : 2 * pad + depth] = low
    return out


def padded(table, rows):
    return np.concatenate([table, np.zeros((rows - table.shape[0],) + table.shape[1:])])


def tables():
    vt, st, ends, w = line_tables()

    def plane(a, first, second, third):
        return np.einsum("i,bj,ck->bcijk", first[a], second, third).reshape(NQ1 * NQ1, MODES)

    face_w = np.outer(w, w).reshape(-1, 1)
    vol_u, vol_p = [], []
    for a in range(NQ1):
        grads = [plane(a, st, vt, vt), plane(a, vt, st, vt), plane(a, vt, vt, st)]
        vol_u.append(np.concatenate([padded(t, PT) for t in [plane(a, vt, vt, vt)] + grads]))
        vol_p.append(padded(np.concatenate([padded(w[a] * face_w * t, PT) for t in grads]), 176))
    eye = np.eye(P1)

    def face(f, tangent):
        e = ends[f % 2][None]
        parts = [e, tangent, tangent] if f < 2 else [tangent, e, tangent] if f < 4 else [tangent, tangent, e]
        out = np.einsum("ai,bj,ck->abcijk", *parts)
        return out.reshape(-1, MODES)

    modal = [padded(face(f, eye), TM) for f in (1, 0, 3, 2, 5, 4)]
    at_points = [padded(face(f, vt), PT) for f in range(6)]
    weighted = [padded(face_w * face(f, vt), PT) for f in range(6)]
    face_u = np.concatenate(modal + at_points)
    face_p = np.concatenate(weighted)
    tangents = padded(np.einsum("bj,ck->bcjk", vt, vt).reshape(NQ1 * NQ1, P1 * P1), 64)
    return (
        np.stack([against_split(t) for t in vol_u]),
        np.stack([against_split(t) for t in vol_p]),
        against_split(face_u),
        against_split(face_p),
        against_split(tangents),
    )


def dot(a, b):
    return lax.dot_general(a, b, (((1,), (0,)), ((), ())), preferred_element_type=F32)


def dot_rows(a, b):
    return lax.dot_general(a, b, (((1,), (1,)), ((), ())), preferred_element_type=F32)


def halves(x):
    high = x.astype(BF16)
    return high, (x - high.astype(F32)).astype(BF16)


def thirds(x):
    high = x.astype(BF16)
    rest = x - high.astype(F32)
    mid = rest.astype(BF16)
    return high, mid, (rest - mid.astype(F32)).astype(BF16)


def digit_sum(m, step, count):
    total = jnp.zeros(m.shape, jnp.int32)
    for n in range(1, count):
        total = total + jnp.where(m >= n * step, 1, 0)
    return total


def top_of(rows):
    m = lax.broadcasted_iota(jnp.int32, (rows, ELEM), 0)
    i = digit_sum(m, P1 * P1, P1)
    m = m - i * (P1 * P1)
    j = digit_sum(m, P1, P1)
    k = m - j * P1
    return jnp.maximum(jnp.maximum(i, j), k)


def factor_top(rows):
    m = lax.broadcasted_iota(jnp.int32, (rows, ELEM), 0)
    d = digit_sum(m, P1 * P1, 3)
    m = m - d * (P1 * P1)
    i = digit_sum(m, P1, P1)
    j = m - i * P1
    return jnp.maximum(i, j)


def speed(values, lead):
    return lead * lax.rsqrt(1.0 + values * values)


def work(
    state,
    adjoint_hbm,
    factors,
    order,
    marks,
    neighbours,
    owner,
    vol_u_hbm,
    vol_p_hbm,
    face_u_hbm,
    face_p_hbm,
    tangents,
    recv,
    recv_rest,
    share,
    adjoint,
    vol_u,
    vol_p,
    face_u,
    face_p,
    send,
    send_rest,
    sel,
    top,
    padded_x,
    fac,
    fac3,
    us,
    ps,
    hsend,
    outer,
    own,
    own_p,
    vals,
    vals_p,
    near,
    gath,
    leaf_sum,
    row_sum,
    grp_sum,
    load_sem,
    self_sem,
    send_sem,
    recv_sem,
    halo_send,
    halo_recv,
    leaf_send,
    leaf_recv,
    row_send,
    row_recv,
    sum_send,
    sum_recv,
):
    g = lax.axis_index("grp")
    r = lax.axis_index("dom")
    lane = lax.rem(r, LEAF)
    row = r // LEAF
    after = lax.rem(r + 1, DOM)
    before = lax.rem(r + DOM - 1, DOM)

    barrier = pltpu.get_barrier_semaphore()

    def greet(to_g, to_r):
        pl.semaphore_signal(barrier, inc=1, device_id=(to_g, to_r), device_id_type=MESH)

    @pl.loop(1, GRP)
    def _(k):
        greet(lax.rem(g + k, GRP), r)

    @pl.loop(1, LEAF)
    def _(k):
        greet(g, row * LEAF + lax.rem(lane + k, LEAF))

    @pl.loop(1, ROWS)
    def _(k):
        greet(g, lax.rem(row + k, ROWS) * LEAF + lane)

    greet(g, after)
    greet(g, before)
    greeted = GRP + LEAF + ROWS - 1

    loads = [
        pltpu.make_async_copy(source, target, load_sem.at[n])
        for n, (source, target) in enumerate(
            (
                (adjoint_hbm, adjoint),
                (face_u_hbm, face_u),
                (vol_u_hbm, vol_u),
                (vol_p_hbm, vol_p),
                (face_p_hbm, face_p),
            )
        )
    ]
    for load in loads:
        load.start()

    to = owner[...]
    hits = jnp.where(lax.broadcasted_iota(jnp.int32, (GRP, ELEM), 0) == to, 1.0, 0.0)
    earlier = jnp.where(
        lax.broadcasted_iota(jnp.int32, (ELEM, ELEM), 0)
        < lax.broadcasted_iota(jnp.int32, (ELEM, ELEM), 1),
        1.0,
        0.0,
    ).astype(BF16)
    counts = dot(hits.astype(BF16), earlier)
    rank = jnp.sum(hits * counts, axis=0, keepdims=True).astype(jnp.int32)
    slot = to * CAP + rank
    sel[...] = jnp.where(
        lax.broadcasted_iota(jnp.int32, (SLOTS, ELEM), 0) == slot, 1.0, 0.0
    ).astype(BF16)

    level = order[...]
    fresh = jnp.clip(level + marks[...], 1, PMAX)
    low = jnp.minimum(level, fresh)
    top[...] = top_of(MPAD)

    for d in range(3):
        for i in range(P1):
            at = (d * P1 + i) * P1
            fac[at : at + P1, :] = factors[d, i]
    fac[FROWS - 1 : 80, :] = jnp.zeros((80 - FROWS + 1, ELEM), F32)
    rows = lax.broadcasted_iota(jnp.int32, (80, ELEM), 0)
    kept = jnp.where(factor_top(80) <= low, fac[...], 0.0)
    fac[...] = jnp.where(rows == FROWS - 1, fresh.astype(F32), kept)
    for n in range(2 * NV):
        fac3[n, 0:SPARE, :] = fac[n * SPARE : (n + 1) * SPARE, :]

    def pack(source, v, most, column):
        padded_x[0:MODES, :] = jnp.where(top[0:MODES, :] <= most, source[v], 0.0)
        padded_x[MODES:MPAD, :] = fac3[column, 0:SPARE, :]
        high, mid, tail = thirds(padded_x[...])
        chosen = sel[...]
        send[column] = dot_rows(chosen, high) + dot_rows(chosen, mid) + dot_rows(chosen, tail)

    def copy_to(c, j):
        first, count = CHUNKS[c]
        ahead = lax.rem(j, 2) * ((j + 1) // 2) + (1 - lax.rem(j, 2)) * (GRP - j // 2)
        to_g = lax.rem(g + ahead, GRP)
        return pltpu.make_async_remote_copy(
            src_ref=send.at[pl.ds(first, count), pl.ds(to_g * CAP, CAP)],
            dst_ref=recv.at[pl.ds(first, count), pl.ds(g * CAP, CAP)],
            send_sem=send_sem.at[c, j],
            recv_sem=recv_sem.at[c, j],
            device_id=(to_g, r),
            device_id_type=MESH,
        )

    def rest_to(j):
        ahead = lax.rem(j, 2) * ((j + 1) // 2) + (1 - lax.rem(j, 2)) * (GRP - j // 2)
        to_g = lax.rem(g + ahead, GRP)
        return pltpu.make_async_remote_copy(
            src_ref=send_rest.at[pl.ds(to_g * 8, 8)],
            dst_ref=recv_rest.at[pl.ds(g * 8, 8)],
            send_sem=send_sem.at[len(CHUNKS), j],
            recv_sem=recv_sem.at[len(CHUNKS), j],
            device_id=(to_g, r),
            device_id_type=MESH,
        )

    def self_copy(c):
        first, count = CHUNKS[c]
        return pltpu.make_async_copy(
            send.at[pl.ds(first, count), pl.ds(g * CAP, CAP)],
            recv.at[pl.ds(first, count), pl.ds(g * CAP, CAP)],
            self_sem.at[c],
        )

    def self_rest():
        return pltpu.make_async_copy(
            send_rest.at[pl.ds(g * 8, 8)], recv_rest.at[pl.ds(g * 8, 8)], self_sem.at[len(CHUNKS)]
        )

    def send_chunk(c):
        @pl.loop(1, GRP)
        def _(j):
            copy_to(c, j).start()

        self_copy(c).start()

    pack(state, 0, low, 0)
    pl.semaphore_wait(barrier, greeted)
    send_chunk(0)

    def split_into(target, source, v, most):
        padded_x[0:MODES, :] = jnp.where(top[0:MODES, :] <= most, source[v], 0.0)
        padded_x[MODES:MPAD, :] = jnp.zeros((SPARE, ELEM), F32)
        high, tail = halves(padded_x[...])
        target[v, 0:MPAD, :] = high
        target[v, MPAD : 2 * MPAD, :] = tail
        target[v, 2 * MPAD :, :] = high

    loads[1].wait()

    @pl.loop(0, NV)
    def _(v):
        split_into(us, state, v, level)
        both = dot(face_u[...], us[v])
        place = pl.ds(pl.multiple_of(v * TM, TM), TM)
        for b in range(4):
            outer[b, place, :] = both[b * TM : (b + 1) * TM]
        hsend[0, place, :] = both[4 * TM : 5 * TM]
        hsend[1, place, :] = both[5 * TM : 6 * TM]
        for f in range(6):
            own[f, v] = both[6 * TM + f * PT : 6 * TM + (f + 1) * PT]

    halos = [
        pltpu.make_async_remote_copy(
            src_ref=hsend.at[n],
            dst_ref=outer.at[4 + n],
            send_sem=halo_send.at[n],
            recv_sem=halo_recv.at[n],
            device_id=(g, to_r),
            device_id_type=MESH,
        )
        for n, to_r in enumerate((after, before))
    ]
    for halo in halos:
        halo.start()

    @pl.loop(1, 4)
    def _(v):
        pack(state, v, low, v)

    send_chunk(1)
    loads[0].wait()

    @pl.loop(4, NV)
    def _(v):
        pack(state, v, low, v)

    @pl.loop(0, 2)
    def _(v):
        pack(adjoint, v, fresh, v + NV)

    send_chunk(2)

    @pl.loop(2, NV)
    def _(v):
        pack(adjoint, v, fresh, v + NV)

    total_rest = jnp.zeros((GRP * 8, MPAD), F32)
    line = lax.broadcasted_iota(jnp.int32, (GRP * 8, ELEM), 0)
    line_slot = (line // 8) * CAP + lax.rem(line, 8)
    from_row = 2 * NV * SPARE - REST_AT
    rest = fac[from_row : from_row + REST + 8, :]
    rest = jnp.concatenate([rest, jnp.zeros((MPAD - REST - 8, ELEM), F32)], axis=0)
    rest = jnp.where(lax.broadcasted_iota(jnp.int32, (MPAD, ELEM), 0) < REST_AT, 0.0, rest)
    for part in range(3):
        chosen = jnp.where(line_slot + 8 * part == slot, 1.0, 0.0).astype(BF16)
        moved = rest if part == 0 else pltpu.roll(rest, REST * part, 0)
        for piece in thirds(moved):
            total_rest = total_rest + dot_rows(chosen, piece)
    send_rest[...] = total_rest

    @pl.loop(1, GRP)
    def _(j):
        rest_to(j).start()

    self_rest().start()
    send_chunk(3)

    @pl.loop(0, NV)
    def _(v):
        split_into(ps, adjoint, v, level + 1)

    loads[2].wait()
    loads[3].wait()
    near[...] = jnp.zeros(near.shape, F32)

    @pl.loop(0, NQ1)
    def _(a):
        @pl.loop(0, NV)
        def _(v):
            vals[v] = dot(vol_u[a], us[v])
            vals_p[v] = dot(vol_p[a], ps[v])

        @pl.loop(0, PT // 8)
        def _(t):
            def at(table, v):
                return vals[v, pl.ds(pl.multiple_of(table * PT + t * 8, 8), 8), :]

            def at_p(table, v):
                return vals_p[v, pl.ds(pl.multiple_of(table * PT + t * 8, 8), 8), :]

            u0 = at(0, 0)
            inverse = lax.rsqrt(1.0 + u0 * u0)
            c = [at(0, 1 + d) * inverse for d in range(3)]
            u5 = at(0, 5)
            soft = jnp.maximum(u5, 0.0) + jnp.log1p(jnp.exp(-jnp.abs(u5)))
            nu = 0.05 + 0.1 * soft
            total = jnp.zeros((8, ELEM), F32)
            for v in range(NV):
                w = [at_p(d, v) for d in range(3)]
                carried = w[0] * c[0] + w[1] * c[1] + w[2] * c[2]
                spread = w[0] * at(1, v) + w[1] * at(2, v) + w[2] * at(3, v)
                total = total + (carried * at(0, v) - nu * spread)
            near[...] = near[...] - total

    loads[4].wait()

    @pl.loop(0, NV)
    def _(v):
        both = dot(face_p[...], ps[v])
        for f in range(6):
            own_p[f, v] = both[f * PT : (f + 1) * PT]

    for halo in halos:
        halo.wait()

    @pl.loop(0, 6)
    def _(f):
        absent = jnp.where(f == 4, jnp.where(r == 0, 1, 0), 0) + jnp.where(
            f == 5, jnp.where(r == DOM - 1, 1, 0), 0
        )
        present = 1.0 - absent.astype(F32)
        high, tail = halves(outer[f] * present)
        source = lax.broadcasted_iota(jnp.int32, (ELEM, ELEM), 0)
        pick = jnp.where(source == neighbours[pl.ds(f, 1), :], 1.0, 0.0).astype(BF16)
        got_high = dot(high, pick).astype(BF16)
        got_tail = dot(tail, pick).astype(BF16)
        for v in range(NV):
            lanes = slice(v * ELEM, (v + 1) * ELEM)
            gath[0:TM, lanes] = got_high[v * TM : (v + 1) * TM]
            gath[TM : 2 * TM, lanes] = got_tail[v * TM : (v + 1) * TM]
            gath[2 * TM :, lanes] = got_high[v * TM : (v + 1) * TM]
        seen = dot(tangents[...], gath[...])
        o = [seen[0:PT, v * ELEM : (v + 1) * ELEM] for v in range(NV)]
        d = f // 2
        sign = (2 * lax.rem(f, 2) - 1).astype(F32)
        lead_o = jnp.where(d == 0, o[1], jnp.where(d == 1, o[2], o[3]))
        half = 0.5 * sign
        speed_t = half * speed(own[f, 0], own[f, 1 + d])
        speed_o = half * speed(o[0], lead_o)
        total = jnp.zeros((PT, ELEM), F32)
        for v in range(NV):
            t = own[f, v]
            total = total + own_p[f, v] * (
                speed_t * t + speed_o * o[v] + 0.5 * (t - o[v])
            )
        part = total[0:8]
        for n in range(1, PT // 8):
            part = part + total[n * 8 : (n + 1) * 8]
        near[...] = near[...] + part

    eta = jnp.abs(jnp.sum(near[...], axis=0, keepdims=True))

    def exchange(buffer, mine, count, send_s, recv_s, device):
        def one(k):
            return pltpu.make_async_remote_copy(
                src_ref=buffer.at[mine],
                dst_ref=buffer.at[mine],
                send_sem=send_s.at[k],
                recv_sem=recv_s.at[k],
                device_id=device(k),
                device_id_type=MESH,
            )

        @pl.loop(1, count)
        def _(k):
            one(k).start()

        @pl.loop(1, count)
        def _(k):
            one(k).wait()

        return jnp.sum(buffer[...], axis=0)

    leaf_sum[lane] = jnp.broadcast_to(jnp.sum(eta, axis=1, keepdims=True), (8, 128))
    part = exchange(
        leaf_sum, lane, LEAF, leaf_send, leaf_recv,
        lambda k: (g, row * LEAF + lax.rem(lane + k, LEAF)),
    )
    row_sum[row] = part
    part = exchange(
        row_sum, row, ROWS, row_send, row_recv,
        lambda k: (g, lax.rem(row + k, ROWS) * LEAF + lane),
    )
    grp_sum[g] = part
    part = exchange(
        grp_sum, g, GRP, sum_send, sum_recv, lambda k: (lax.rem(g + k, GRP), r)
    )
    mean = part[0:1, 0:1] / (ELEM * GRP * DOM)
    share[...] = eta / (mean + 1e-06)

    for c in range(len(CHUNKS)):
        self_copy(c).wait()

        @pl.loop(1, GRP)
        def _(j):
            copy_to(c, j).wait()

    self_rest().wait()

    @pl.loop(1, GRP)
    def _(j):
        rest_to(j).wait()


def unpack(cols_s, cols_p, rest, share_in, moved_state, moved_adjoint, moved_factors, moved_order, share, fac):
    v = pl.program_id(0)
    first = cols_s[0].T
    second = cols_p[0].T
    moved_state[0] = first[0:MODES]
    moved_adjoint[0] = second[0:MODES]
    fac[v, 0:SPARE, :] = first[MODES:MPAD]
    fac[NV + v, 0:SPARE, :] = second[MODES:MPAD]

    @pl.when(v == NV - 1)
    def _():
        lines = rest[...].reshape(GRP, 1, 8, MPAD)
        parts = [lines] + [
            pltpu.roll(rest[...], MPAD - REST * n, 1).reshape(GRP, 1, 8, MPAD) for n in (1, 2)
        ]
        tail = jnp.concatenate(parts, axis=1).reshape(SLOTS, MPAD).T
        rows = [fac[n, 0:SPARE, :] for n in range(2 * NV)] + [tail[REST_AT : REST_AT + REST]]
        whole = jnp.concatenate(rows, axis=0)
        for d in range(3):
            for i in range(P1):
                at = (d * P1 + i) * P1
                moved_factors[d, i] = whole[at : at + P1]
        moved_order[...] = whole[FROWS - 1 : FROWS].astype(jnp.int32)
        share[...] = share_in[...]


def body(state, adjoint, factors, order, marks, neighbours, new_owner):
    vol_u, vol_p, face_u, face_p, tangents = [jnp.asarray(t) for t in tables()]
    vmem = pl.BlockSpec(memory_space=pltpu.VMEM)
    anywhere = pl.BlockSpec(memory_space=pl.ANY)
    dma = pltpu.SemaphoreType.DMA
    chunks = len(CHUNKS) + 1
    recv, recv_rest, share = pl.pallas_call(
        work,
        name="indicator_and_send",
        out_shape=(
            jax.ShapeDtypeStruct((2 * NV, SLOTS, MPAD), F32),
            jax.ShapeDtypeStruct((GRP * 8, MPAD), F32),
            jax.ShapeDtypeStruct((1, ELEM), F32),
        ),
        in_specs=[vmem, anywhere, vmem, vmem, vmem, vmem, vmem]
        + [anywhere] * 4
        + [vmem],
        out_specs=(anywhere, anywhere, vmem),
        scratch_shapes=[
            pltpu.VMEM((NV, MODES, ELEM), F32),
            pltpu.VMEM(vol_u.shape, BF16),
            pltpu.VMEM(vol_p.shape, BF16),
            pltpu.VMEM(face_u.shape, BF16),
            pltpu.VMEM(face_p.shape, BF16),
            pltpu.VMEM((2 * NV, SLOTS, MPAD), F32),
            pltpu.VMEM((GRP * 8, MPAD), F32),
            pltpu.VMEM((SLOTS, ELEM), BF16),
            pltpu.VMEM((MPAD, ELEM), jnp.int32),
            pltpu.VMEM((MPAD, ELEM), F32),
            pltpu.VMEM((80, ELEM), F32),
            pltpu.VMEM((2 * NV, 8, ELEM), F32),
            pltpu.VMEM((NV, KCAT, ELEM), BF16),
            pltpu.VMEM((NV, KCAT, ELEM), BF16),
            pltpu.VMEM((2, NV * TM, ELEM), F32),
            pltpu.VMEM((6, NV * TM, ELEM), F32),
            pltpu.VMEM((6, NV, PT, ELEM), F32),
            pltpu.VMEM((6, NV, PT, ELEM), F32),
            pltpu.VMEM((NV, 4 * PT, ELEM), F32),
            pltpu.VMEM((NV, 176, ELEM), F32),
            pltpu.VMEM((8, ELEM), F32),
            pltpu.VMEM((3 * TM, NV * ELEM), BF16),
            pltpu.VMEM((LEAF, 8, 128), F32),
            pltpu.VMEM((ROWS, 8, 128), F32),
            pltpu.VMEM((GRP, 8, 128), F32),
            dma((5,)),
            dma((chunks,)),
            dma((chunks, GRP)),
            dma((chunks, GRP)),
            dma((2,)),
            dma((2,)),
            dma((LEAF,)),
            dma((LEAF,)),
            dma((ROWS,)),
            dma((ROWS,)),
            dma((GRP,)),
            dma((GRP,)),
        ],
        compiler_params=pltpu.CompilerParams(
            collective_id=0, has_side_effects=True, vmem_limit_bytes=48 << 20
        ),
    )(
        state,
        adjoint,
        factors,
        order.reshape(1, ELEM),
        marks.reshape(1, ELEM),
        neighbours,
        new_owner.reshape(1, ELEM),
        vol_u,
        vol_p,
        face_u,
        face_p,
        tangents,
    )
    moved_state, moved_adjoint, moved_factors, moved_order, share = pl.pallas_call(
        unpack,
        name="unpack_slots",
        grid=(NV,),
        out_shape=(
            jax.ShapeDtypeStruct((NV, MODES, SLOTS), F32),
            jax.ShapeDtypeStruct((NV, MODES, SLOTS), F32),
            jax.ShapeDtypeStruct((3, P1, P1, SLOTS), F32),
            jax.ShapeDtypeStruct((1, SLOTS), jnp.int32),
            jax.ShapeDtypeStruct((1, ELEM), F32),
        ),
        in_specs=[
            pl.BlockSpec((1, SLOTS, MPAD), lambda v: (v, 0, 0)),
            pl.BlockSpec((1, SLOTS, MPAD), lambda v: (v + NV, 0, 0)),
            pl.BlockSpec((GRP * 8, MPAD), lambda v: (0, 0)),
            pl.BlockSpec((1, ELEM), lambda v: (0, 0)),
        ],
        out_specs=(
            pl.BlockSpec((1, MODES, SLOTS), lambda v: (v, 0, 0)),
            pl.BlockSpec((1, MODES, SLOTS), lambda v: (v, 0, 0)),
            pl.BlockSpec((3, P1, P1, SLOTS), lambda v: (0, 0, 0, 0)),
            pl.BlockSpec((1, SLOTS), lambda v: (0, 0)),
            pl.BlockSpec((1, ELEM), lambda v: (0, 0)),
        ),
        scratch_shapes=[pltpu.VMEM((2 * NV, 8, SLOTS), F32)],
        compiler_params=pltpu.CompilerParams(vmem_limit_bytes=16 << 20),
    )(recv, recv, recv_rest, share)
    return (
        share.reshape(ELEM),
        moved_state,
        moved_adjoint,
        moved_factors,
        moved_order.reshape(SLOTS),
    )


def solution(mesh):
    return jax.shard_map(
        body,
        mesh=mesh,
        in_specs=(
            P(None, None, ("grp", "dom")),
            P(None, None, ("grp", "dom")),
            P(None, None, None, ("grp", "dom")),
            P(("grp", "dom")),
            P(("grp", "dom")),
            P(None, ("grp", "dom")),
            P(("grp", "dom"), None),
        ),
        out_specs=(
            P(("grp", "dom")),
            P(None, None, ("grp", "dom")),
            P(None, None, ("grp", "dom")),
            P(None, None, None, ("grp", "dom")),
            P(("grp", "dom")),
        ),
        check_vma=False,
    )
```

profile of v0, /device:TPU:58, one launch (start us, length us, event | category | flops | bytes accessed | tf_op | source)
XLA Modules:
  0.0 144.4 jit_solution(5564254641199365474)
XLA Ops:
  0.6 0.9 copy.17.factors
  1.6 0.0 copy-start.1
  1.6 1.3 copy-done.1
  2.8 0.0 copy-start.2
  2.8 1.2 copy-done.2
  4.0 0.0 copy-start.3
  4.0 1.1 copy-done.3
  5.2 0.0 copy-start.4
  5.2 1.1 copy-done.4
  6.3 0.0 copy-start.5
  6.3 1.0 copy-done.5
  7.3 0.0 copy-start.6
  7.3 0.9 copy-done.6
  8.2 0.0 copy-start.7
  8.2 0.7 copy-done.7
  9.0 0.0 copy-start.8
  9.0 0.7 copy-done.8
  9.7 0.0 copy-start.9
  9.7 0.7 copy-done.9
  10.3 0.0 copy-start.10
  10.3 0.7 copy-done.10
  11.0 0.0 copy-start.11
  11.0 0.7 copy-done.11
  11.7 126.6 %indicator_and_send.1 = (f32[12,384,128]{2,1,0:T(8,128)}, f32[128,128]{1,0:T(8,128)S(1)}, f32[1,256]{1,0:T(1,128)S(1)}) custom-call(f32[6,125,256]{2,1,0:T(8,128)S(1)} %copy-done.3, f32[6,125,256]{2,1,0:T(8,128)S(1)} %copy-done.4, f32[3,5,5,256]{3,2,1,0:T(8,128)S(1)} %copy.17.factors, s32[1,256]{1,0:T(1,128)S(1)} %bitcast.4, s32[1,256]{1,0:T(1,128)S(1)} %bitcast.5, ...), custom_call_target="tpu_custom_call" | custom-call | tf_op jit(solution)/shard_map/indicator_and_send/pallas_call | solution.py:591
  138.3 0.0 copy-start
  138.4 1.7 %copy-done = f32[12,384,128]{2,1,0:T(8,128)S(1)} copy-done((f32[12,384,128]{2,1,0:T(8,128)S(1)}, f32[12,384,128]{2,1,0:T(8,128)}, u32[]{:S(2)}) %copy-start) | copy-done | bytes 2359320
  140.0 3.1 %unpack_slots.1 = (f32[6,125,384]{2,1,0:T(8,128)}, f32[6,125,384]{2,1,0:T(8,128)}, f32[3,5,5,384]{3,2,1,0:T(8,128)S(1)}, s32[1,384]{1,0:T(1,128)S(1)}, f32[1,256]{1,0:T(1,128)}) custom-call(f32[12,384,128]{2,1,0:T(8,128)S(1)} %copy-done, f32[12,384,128]{2,1,0:T(8,128)S(1)} %copy-done, f32[128,128]{1,0:T(8,128)S(1)} %get-tuple-element.14.rest, ...), custom_call_target="tpu_custom_call" | custom-call | tf_op jit(solution)/shard_map/unpack_slots/pallas_call | solution.py:659
  143.1 0.6 reduce
  143.7 0.7 copy.18
Async XLA Ops:
  1.6 1.3 copy-start.1
  2.8 1.2 copy-start.2
  4.0 1.1 copy-start.3
  5.2 1.1 copy-start.4
  6.3 1.0 copy-start.5
  7.3 0.9 copy-start.6
  8.2 0.7 copy-start.7
  9.0 0.7 copy-start.8
  9.7 0.7 copy-start.9
  10.3 0.7 copy-start.10
  11.0 0.7 copy-start.11
  138.3 1.7 %copy-start = (f32[12,384,128]{2,1,0:T(8,128)S(1)}, f32[12,384,128]{2,1,0:T(8,128)}, u32[]{:S(2)}) copy-start(f32[12,384,128]{2,1,0:T(8,128)} %get-tuple-element.13.cols_s.cols_p) | copy-start | bytes 7077892
where the time goes:
time: 145 us; the launch traced here: 144 us
  Pallas kernels  130 us (90%)
  local copies, waits for them, and re-layouts  13.4 us (9%)
    pallas_call x1, Pallas kernels, body(): pl.pallas_call(work, name='indicator_and_send', out_shape=(jax.ShapeDtype...  127 us
    unnamed x26, local copies, waits for them, and re-layouts  13.4 us
    pallas_call x1, Pallas kernels, body(): pl.pallas_call(unpack, name='unpack_slots', grid=(NV,), out_shape=(jax.Sh...  3.06 us

commit v1 on v0

--- a/solution.py
+++ b/solution.py
@@ -31,7 +31,11 @@
 REST = FROWS - 2 * NV * SPARE
 REST_AT = 2 * NV * SPARE % 8
 MESH = pl.DeviceIdType.MESH
-CHUNKS = ((0, 1), (1, 3), (4, 4), (8, 4))
+COLS = 2 * NV
+BLOCK = COLS * CAP + 8
+PIECES = ((0, 1), (1, 2), (3, 3), (6, 3), (9, 3))
+NEAR = 2
+BEFORE = 4
 F32 = jnp.float32
 BF16 = jnp.bfloat16
 
@@ -146,10 +150,8 @@
 
 def factor_top(rows):
     m = lax.broadcasted_iota(jnp.int32, (rows, ELEM), 0)
-    d = digit_sum(m, P1 * P1, 3)
-    m = m - d * (P1 * P1)
-    i = digit_sum(m, P1, P1)
-    j = m - i * P1
+    i = digit_sum(m, 3 * P1, P1)
+    j = digit_sum(m - i * (3 * P1), 3, P1)
     return jnp.maximum(i, j)
 
 
@@ -158,28 +160,33 @@
 
 
 def work(
-    state,
+    state_hbm,
     adjoint_hbm,
-    factors,
-    order,
-    marks,
-    neighbours,
-    owner,
+    factors_hbm,
+    order_hbm,
+    marks_hbm,
+    neighbours_hbm,
+    owner_hbm,
     vol_u_hbm,
     vol_p_hbm,
     face_u_hbm,
     face_p_hbm,
+    tangents_hbm,
+    recv,
+    share,
+    owner,
+    order,
+    marks,
+    state,
+    factors,
+    adjoint,
+    neighbours,
     tangents,
-    recv,
-    recv_rest,
-    share,
-    adjoint,
     vol_u,
     vol_p,
     face_u,
     face_p,
     send,
-    send_rest,
     sel,
     top,
     padded_x,
@@ -243,8 +250,15 @@
         pltpu.make_async_copy(source, target, load_sem.at[n])
         for n, (source, target) in enumerate(
             (
+                (owner_hbm, owner),
+                (order_hbm, order),
+                (marks_hbm, marks),
+                (state_hbm, state),
+                (factors_hbm, factors),
                 (adjoint_hbm, adjoint),
                 (face_u_hbm, face_u),
+                (neighbours_hbm, neighbours),
+                (tangents_hbm, tangents),
                 (vol_u_hbm, vol_u),
                 (vol_p_hbm, vol_p),
                 (face_p_hbm, face_p),
@@ -253,6 +267,8 @@
     ]
     for load in loads:
         load.start()
+    for load in loads[:5]:
+        load.wait()
 
     to = owner[...]
     hits = jnp.where(lax.broadcasted_iota(jnp.int32, (GRP, ELEM), 0) == to, 1.0, 0.0)
@@ -274,10 +290,10 @@
     low = jnp.minimum(level, fresh)
     top[...] = top_of(MPAD)
 
-    for d in range(3):
-        for i in range(P1):
-            at = (d * P1 + i) * P1
-            fac[at : at + P1, :] = factors[d, i]
+    for i in range(P1):
+        for j in range(P1):
+            at = (i * P1 + j) * 3
+            fac[at : at + 3, :] = factors[i, j]
     fac[FROWS - 1 : 80, :] = jnp.zeros((80 - FROWS + 1, ELEM), F32)
     rows = lax.broadcasted_iota(jnp.int32, (80, ELEM), 0)
     kept = jnp.where(factor_top(80) <= low, fac[...], 0.0)
@@ -290,56 +306,79 @@
         padded_x[MODES:MPAD, :] = fac3[column, 0:SPARE, :]
         high, mid, tail = thirds(padded_x[...])
         chosen = sel[...]
-        send[column] = dot_rows(chosen, high) + dot_rows(chosen, mid) + dot_rows(chosen, tail)
-
-    def copy_to(c, j):
-        first, count = CHUNKS[c]
-        ahead = lax.rem(j, 2) * ((j + 1) // 2) + (1 - lax.rem(j, 2)) * (GRP - j // 2)
-        to_g = lax.rem(g + ahead, GRP)
+        out = dot_rows(chosen, tail) + dot_rows(chosen, mid) + dot_rows(chosen, high)
+        place = pl.ds(pl.multiple_of(column * CAP, 8), CAP)
+        send[:, place, :] = out.reshape(GRP, CAP, MPAD)
+
+    def pack_rest():
+        total = jnp.zeros((GRP * 8, MPAD), F32)
+        line = lax.broadcasted_iota(jnp.int32, (GRP * 8, ELEM), 0)
+        line_slot = (line // 8) * CAP + lax.rem(line, 8)
+        from_row = 2 * NV * SPARE - REST_AT
+        rest = fac[from_row : from_row + REST + 8, :]
+        rest = jnp.concatenate([rest, jnp.zeros((MPAD - REST - 8, ELEM), F32)], axis=0)
+        rest = jnp.where(lax.broadcasted_iota(jnp.int32, (MPAD, ELEM), 0) < REST_AT, 0.0, rest)
+        for part in range(3):
+            chosen = jnp.where(line_slot + 8 * part == slot, 1.0, 0.0).astype(BF16)
+            moved = rest if part == 0 else pltpu.roll(rest, REST * part, 0)
+            for piece in reversed(thirds(moved)):
+                total = total + dot_rows(chosen, piece)
+        send[:, COLS * CAP : BLOCK, :] = total.reshape(GRP, 8, MPAD)
+
+    def block_to(ahead, n, first, count):
+        to_g = lax.rem(g + ahead + GRP, GRP)
+        rows = pl.ds(first, count)
         return pltpu.make_async_remote_copy(
-            src_ref=send.at[pl.ds(first, count), pl.ds(to_g * CAP, CAP)],
-            dst_ref=recv.at[pl.ds(first, count), pl.ds(g * CAP, CAP)],
-            send_sem=send_sem.at[c, j],
-            recv_sem=recv_sem.at[c, j],
+            src_ref=send.at[to_g, rows],
+            dst_ref=recv.at[g, rows],
+            send_sem=send_sem.at[n],
+            recv_sem=recv_sem.at[n],
             device_id=(to_g, r),
             device_id_type=MESH,
         )
 
-    def rest_to(j):
-        ahead = lax.rem(j, 2) * ((j + 1) // 2) + (1 - lax.rem(j, 2)) * (GRP - j // 2)
-        to_g = lax.rem(g + ahead, GRP)
-        return pltpu.make_async_remote_copy(
-            src_ref=send_rest.at[pl.ds(to_g * 8, 8)],
-            dst_ref=recv_rest.at[pl.ds(g * 8, 8)],
-            send_sem=send_sem.at[len(CHUNKS), j],
-            recv_sem=recv_sem.at[len(CHUNKS), j],
-            device_id=(to_g, r),
-            device_id_type=MESH,
-        )
-
-    def self_copy(c):
-        first, count = CHUNKS[c]
-        return pltpu.make_async_copy(
-            send.at[pl.ds(first, count), pl.ds(g * CAP, CAP)],
-            recv.at[pl.ds(first, count), pl.ds(g * CAP, CAP)],
-            self_sem.at[c],
-        )
-
-    def self_rest():
-        return pltpu.make_async_copy(
-            send_rest.at[pl.ds(g * 8, 8)], recv_rest.at[pl.ds(g * 8, 8)], self_sem.at[len(CHUNKS)]
-        )
-
-    def send_chunk(c):
-        @pl.loop(1, GRP)
-        def _(j):
-            copy_to(c, j).start()
-
-        self_copy(c).start()
-
-    pack(state, 0, low, 0)
-    pl.semaphore_wait(barrier, greeted)
-    send_chunk(0)
+    partners = [k for d in range(1, GRP // 2) for k in (d, -d)] + [GRP // 2]
+    blocks = {}
+    for k in partners:
+        n = len(blocks) if not blocks else max(blocks.values(), key=lambda x: x[-1][1])[-1][1] + 1
+        if abs(k) <= NEAR:
+            cut = [0] + [(c + count) * CAP for c, count in PIECES[:-1]] + [BLOCK]
+            blocks[k] = [(p, n + p, cut[p], cut[p + 1] - cut[p]) for p in range(len(PIECES))]
+        else:
+            blocks[k] = [(0, n, 0, BLOCK)]
+
+    def send_block(k, p=0):
+        block_to(k, *blocks[k][p][1:]).start()
+
+    def send_piece(p):
+        for k in partners:
+            if abs(k) <= NEAR:
+                send_block(k, p)
+
+    own_block = pltpu.make_async_copy(send.at[g], recv.at[g], self_sem)
+
+    def pack_columns(first, count):
+        @pl.loop(first, min(first + count, NV))
+        def _(c):
+            pack(state, c, low, c)
+
+        @pl.loop(max(first, NV), first + count)
+        def _(c):
+            pack(adjoint, c - NV, fresh, c)
+
+    for p, (first, count) in enumerate(PIECES):
+        if first <= NV < first + count or first == NV:
+            loads[5].wait()
+        pack_columns(first, count)
+        if p == 0:
+            pl.semaphore_wait(barrier, greeted)
+        if p == len(PIECES) - 1:
+            pack_rest()
+        send_piece(p)
+    for k in partners:
+        if NEAR < abs(k) <= BEFORE:
+            send_block(k)
+    own_block.start()
 
     def split_into(target, source, v, most):
         padded_x[0:MODES, :] = jnp.where(top[0:MODES, :] <= most, source[v], 0.0)
@@ -349,7 +388,7 @@
         target[v, MPAD : 2 * MPAD, :] = tail
         target[v, 2 * MPAD :, :] = high
 
-    loads[1].wait()
+    loads[6].wait()
 
     @pl.loop(0, NV)
     def _(v):
@@ -377,54 +416,12 @@
     for halo in halos:
         halo.start()
 
-    @pl.loop(1, 4)
-    def _(v):
-        pack(state, v, low, v)
-
-    send_chunk(1)
-    loads[0].wait()
-
-    @pl.loop(4, NV)
-    def _(v):
-        pack(state, v, low, v)
-
-    @pl.loop(0, 2)
-    def _(v):
-        pack(adjoint, v, fresh, v + NV)
-
-    send_chunk(2)
-
-    @pl.loop(2, NV)
-    def _(v):
-        pack(adjoint, v, fresh, v + NV)
-
-    total_rest = jnp.zeros((GRP * 8, MPAD), F32)
-    line = lax.broadcasted_iota(jnp.int32, (GRP * 8, ELEM), 0)
-    line_slot = (line // 8) * CAP + lax.rem(line, 8)
-    from_row = 2 * NV * SPARE - REST_AT
-    rest = fac[from_row : from_row + REST + 8, :]
-    rest = jnp.concatenate([rest, jnp.zeros((MPAD - REST - 8, ELEM), F32)], axis=0)
-    rest = jnp.where(lax.broadcasted_iota(jnp.int32, (MPAD, ELEM), 0) < REST_AT, 0.0, rest)
-    for part in range(3):
-        chosen = jnp.where(line_slot + 8 * part == slot, 1.0, 0.0).astype(BF16)
-        moved = rest if part == 0 else pltpu.roll(rest, REST * part, 0)
-        for piece in thirds(moved):
-            total_rest = total_rest + dot_rows(chosen, piece)
-    send_rest[...] = total_rest
-
-    @pl.loop(1, GRP)
-    def _(j):
-        rest_to(j).start()
-
-    self_rest().start()
-    send_chunk(3)
-
     @pl.loop(0, NV)
     def _(v):
         split_into(ps, adjoint, v, level + 1)
 
-    loads[2].wait()
-    loads[3].wait()
+    loads[9].wait()
+    loads[10].wait()
     near[...] = jnp.zeros(near.shape, F32)
 
     @pl.loop(0, NQ1)
@@ -456,7 +453,9 @@
                 total = total + (carried * at(0, v) - nu * spread)
             near[...] = near[...] - total
 
-    loads[4].wait()
+    loads[11].wait()
+    loads[7].wait()
+    loads[8].wait()
 
     @pl.loop(0, NV)
     def _(v):
@@ -504,7 +503,7 @@
 
     eta = jnp.abs(jnp.sum(near[...], axis=0, keepdims=True))
 
-    def exchange(buffer, mine, count, send_s, recv_s, device):
+    def exchange(buffer, mine, count, send_s, recv_s, device, then):
         def one(k):
             return pltpu.make_async_remote_copy(
                 src_ref=buffer.at[mine],
@@ -519,6 +518,10 @@
         def _(k):
             one(k).start()
 
+        for k in partners:
+            if abs(k) in then:
+                send_block(k)
+
         @pl.loop(1, count)
         def _(k):
             one(k).wait()
@@ -529,85 +532,116 @@
     part = exchange(
         leaf_sum, lane, LEAF, leaf_send, leaf_recv,
         lambda k: (g, row * LEAF + lax.rem(lane + k, LEAF)),
+        (BEFORE + 1,),
     )
     row_sum[row] = part
     part = exchange(
         row_sum, row, ROWS, row_send, row_recv,
         lambda k: (g, lax.rem(row + k, ROWS) * LEAF + lane),
+        (BEFORE + 2,),
     )
     grp_sum[g] = part
     part = exchange(
-        grp_sum, g, GRP, sum_send, sum_recv, lambda k: (lax.rem(g + k, GRP), r)
+        grp_sum, g, GRP, sum_send, sum_recv, lambda k: (lax.rem(g + k, GRP), r),
+        range(BEFORE + 3, GRP),
     )
     mean = part[0:1, 0:1] / (ELEM * GRP * DOM)
     share[...] = eta / (mean + 1e-06)
 
-    for c in range(len(CHUNKS)):
-        self_copy(c).wait()
-
-        @pl.loop(1, GRP)
-        def _(j):
-            copy_to(c, j).wait()
-
-    self_rest().wait()
-
-    @pl.loop(1, GRP)
-    def _(j):
-        rest_to(j).wait()
-
-
-def unpack(cols_s, cols_p, rest, share_in, moved_state, moved_adjoint, moved_factors, moved_order, share, fac):
-    v = pl.program_id(0)
-    first = cols_s[0].T
-    second = cols_p[0].T
-    moved_state[0] = first[0:MODES]
-    moved_adjoint[0] = second[0:MODES]
-    fac[v, 0:SPARE, :] = first[MODES:MPAD]
-    fac[NV + v, 0:SPARE, :] = second[MODES:MPAD]
-
-    @pl.when(v == NV - 1)
-    def _():
-        lines = rest[...].reshape(GRP, 1, 8, MPAD)
-        parts = [lines] + [
-            pltpu.roll(rest[...], MPAD - REST * n, 1).reshape(GRP, 1, 8, MPAD) for n in (1, 2)
-        ]
-        tail = jnp.concatenate(parts, axis=1).reshape(SLOTS, MPAD).T
-        rows = [fac[n, 0:SPARE, :] for n in range(2 * NV)] + [tail[REST_AT : REST_AT + REST]]
-        whole = jnp.concatenate(rows, axis=0)
-        for d in range(3):
-            for i in range(P1):
-                at = (d * P1 + i) * P1
-                moved_factors[d, i] = whole[at : at + P1]
-        moved_order[...] = whole[FROWS - 1 : FROWS].astype(jnp.int32)
-        share[...] = share_in[...]
+    own_block.wait()
+    for k in partners:
+        for piece in blocks[k]:
+            block_to(k, *piece[1:]).wait()
+
+
+def unpack(
+    recv,
+    share_in,
+    moved_state,
+    moved_adjoint,
+    moved_factors,
+    moved_order,
+    share,
+    columns,
+    spare,
+    factors,
+    order,
+    sem,
+):
+    copies = []
+
+    def put(source, target):
+        copy = pltpu.make_async_copy(source, target, sem.at[len(copies)])
+        copy.start()
+        copies.append(copy)
+
+    put(share_in, share)
+    for c in range(COLS):
+        lines = recv[:, c * CAP : (c + 1) * CAP, :].reshape(SLOTS, MPAD).T
+        columns[c] = lines[0:MODES]
+        spare[c, 0:SPARE, :] = lines[MODES:MPAD]
+        target = moved_state.at[c] if c < NV else moved_adjoint.at[c - NV]
+        put(columns.at[c], target)
+    rest = recv[:, COLS * CAP : BLOCK, :].reshape(GRP * 8, MPAD)
+    parts = [rest] + [pltpu.roll(rest, MPAD - REST * n, 1) for n in (1, 2)]
+    parts = [part.reshape(GRP, 1, 8, MPAD) for part in parts]
+    lines = jnp.concatenate(parts, axis=1).reshape(SLOTS, MPAD).T
+    rows = [spare[c, 0:SPARE, :] for c in range(COLS)]
+    whole = jnp.concatenate(rows + [lines[REST_AT : REST_AT + REST]], axis=0)
+    for i in range(P1):
+        for j in range(P1):
+            at = (i * P1 + j) * 3
+            factors[i, j] = whole[at : at + 3]
+    put(factors, moved_factors)
+    order[...] = whole[FROWS - 1 : FROWS].astype(jnp.int32)
+    put(order, moved_order)
+    for copy in copies:
+        copy.wait()
 
 
 def body(state, adjoint, factors, order, marks, neighbours, new_owner):
     vol_u, vol_p, face_u, face_p, tangents = [jnp.asarray(t) for t in tables()]
+    hbm = pl.BlockSpec(memory_space=pltpu.HBM)
     vmem = pl.BlockSpec(memory_space=pltpu.VMEM)
-    anywhere = pl.BlockSpec(memory_space=pl.ANY)
     dma = pltpu.SemaphoreType.DMA
-    chunks = len(CHUNKS) + 1
-    recv, recv_rest, share = pl.pallas_call(
+    copies = GRP - 1 + 2 * NEAR * (len(PIECES) - 1)
+    arrays = (
+        state,
+        adjoint,
+        factors.transpose(1, 2, 0, 3),
+        order.reshape(1, ELEM),
+        marks.reshape(1, ELEM),
+        neighbours,
+        new_owner.reshape(1, ELEM),
+        vol_u,
+        vol_p,
+        face_u,
+        face_p,
+        tangents,
+    )
+    recv, share = pl.pallas_call(
         work,
         name="indicator_and_send",
         out_shape=(
-            jax.ShapeDtypeStruct((2 * NV, SLOTS, MPAD), F32),
-            jax.ShapeDtypeStruct((GRP * 8, MPAD), F32),
-            jax.ShapeDtypeStruct((1, ELEM), F32),
+            pltpu.VMEM((GRP, BLOCK, MPAD), F32),
+            pltpu.VMEM((1, ELEM), F32),
         ),
-        in_specs=[vmem, anywhere, vmem, vmem, vmem, vmem, vmem]
-        + [anywhere] * 4
-        + [vmem],
-        out_specs=(anywhere, anywhere, vmem),
+        in_specs=[hbm] * len(arrays),
+        out_specs=(vmem, vmem),
         scratch_shapes=[
+            pltpu.VMEM((1, ELEM), jnp.int32),
+            pltpu.VMEM((1, ELEM), jnp.int32),
+            pltpu.VMEM((1, ELEM), jnp.int32),
             pltpu.VMEM((NV, MODES, ELEM), F32),
+            pltpu.VMEM((P1, P1, 3, ELEM), F32),
+            pltpu.VMEM((NV, MODES, ELEM), F32),
+            pltpu.VMEM((6, ELEM), jnp.int32),
+            pltpu.VMEM(tangents.shape, BF16),
             pltpu.VMEM(vol_u.shape, BF16),
             pltpu.VMEM(vol_p.shape, BF16),
             pltpu.VMEM(face_u.shape, BF16),
             pltpu.VMEM(face_p.shape, BF16),
-            pltpu.VMEM((2 * NV, SLOTS, MPAD), F32),
-            pltpu.VMEM((GRP * 8, MPAD), F32),
+            pltpu.VMEM((GRP, BLOCK, MPAD), F32),
             pltpu.VMEM((SLOTS, ELEM), BF16),
             pltpu.VMEM((MPAD, ELEM), jnp.int32),
             pltpu.VMEM((MPAD, ELEM), F32),
@@ -626,10 +660,10 @@
             pltpu.VMEM((LEAF, 8, 128), F32),
             pltpu.VMEM((ROWS, 8, 128), F32),
             pltpu.VMEM((GRP, 8, 128), F32),
-            dma((5,)),
-            dma((chunks,)),
-            dma((chunks, GRP)),
-            dma((chunks, GRP)),
+            dma((12,)),
+            dma,
+            dma((copies,)),
+            dma((copies,)),
             dma((2,)),
             dma((2,)),
             dma((LEAF,)),
@@ -640,54 +674,35 @@
             dma((GRP,)),
         ],
         compiler_params=pltpu.CompilerParams(
-            collective_id=0, has_side_effects=True, vmem_limit_bytes=48 << 20
+            collective_id=0, has_side_effects=True, vmem_limit_bytes=32 << 20
         ),
-    )(
-        state,
-        adjoint,
-        factors,
-        order.reshape(1, ELEM),
-        marks.reshape(1, ELEM),
-        neighbours,
-        new_owner.reshape(1, ELEM),
-        vol_u,
-        vol_p,
-        face_u,
-        face_p,
-        tangents,
-    )
+    )(*[pltpu.with_memory_space_constraint(x, pltpu.HBM) for x in arrays])
     moved_state, moved_adjoint, moved_factors, moved_order, share = pl.pallas_call(
         unpack,
         name="unpack_slots",
-        grid=(NV,),
         out_shape=(
             jax.ShapeDtypeStruct((NV, MODES, SLOTS), F32),
             jax.ShapeDtypeStruct((NV, MODES, SLOTS), F32),
-            jax.ShapeDtypeStruct((3, P1, P1, SLOTS), F32),
+            jax.ShapeDtypeStruct((P1, P1, 3, SLOTS), F32),
             jax.ShapeDtypeStruct((1, SLOTS), jnp.int32),
             jax.ShapeDtypeStruct((1, ELEM), F32),
         ),
-        in_specs=[
-            pl.BlockSpec((1, SLOTS, MPAD), lambda v: (v, 0, 0)),
-            pl.BlockSpec((1, SLOTS, MPAD), lambda v: (v + NV, 0, 0)),
-            pl.BlockSpec((GRP * 8, MPAD), lambda v: (0, 0)),
-            pl.BlockSpec((1, ELEM), lambda v: (0, 0)),
+        in_specs=[vmem, vmem],
+        out_specs=(hbm,) * 5,
+        scratch_shapes=[
+            pltpu.VMEM((COLS, MODES, SLOTS), F32),
+            pltpu.VMEM((COLS, 8, SLOTS), F32),
+            pltpu.VMEM((P1, P1, 3, SLOTS), F32),
+            pltpu.VMEM((1, SLOTS), jnp.int32),
+            dma((COLS + 3,)),
         ],
-        out_specs=(
-            pl.BlockSpec((1, MODES, SLOTS), lambda v: (v, 0, 0)),
-            pl.BlockSpec((1, MODES, SLOTS), lambda v: (v, 0, 0)),
-            pl.BlockSpec((3, P1, P1, SLOTS), lambda v: (0, 0, 0, 0)),
-            pl.BlockSpec((1, SLOTS), lambda v: (0, 0)),
-            pl.BlockSpec((1, ELEM), lambda v: (0, 0)),
-        ),
-        scratch_shapes=[pltpu.VMEM((2 * NV, 8, SLOTS), F32)],
-        compiler_params=pltpu.CompilerParams(vmem_limit_bytes=16 << 20),
-    )(recv, recv, recv_rest, share)
+        compiler_params=pltpu.CompilerParams(vmem_limit_bytes=24 << 20),
+    )(*[pltpu.with_memory_space_constraint(x, pltpu.VMEM) for x in (recv, share)])
     return (
         share.reshape(ELEM),
         moved_state,
         moved_adjoint,
-        moved_factors,
+        moved_factors.transpose(2, 0, 1, 3),
         moved_order.reshape(SLOTS),
     )
 

time: 145 us -> 129 us (0.89)
  the two profiles are of different devices: /device:TPU:58 before, /device:TPU:32 now
where the time goes in v1:
time: 129 us
  Pallas kernels  128 us (99%)
    pallas_call x1, Pallas kernels, body(): pl.pallas_call(work, name='indicator_and_send', out_shape=(pltpu.VMEM((GR...  126 us

profile of v1, /device:TPU:32, one launch (start us, length us, event | category | flops | bytes accessed | tf_op | source)
XLA Modules:
  0.0 129.3 jit_solution(2405850377234139775)
XLA Ops:
  0.6 126.3 %indicator_and_send.1 = (f32[16,296,128]{2,1,0:T(8,128)S(1)}, f32[1,256]{1,0:T(1,128)S(1)}) custom-call(f32[6,125,256]{2,1,0:T(8,128)} %state_hbm.1, f32[6,125,256]{2,1,0:T(8,128)} %adjoint_hbm.1, f32[5,5,3,256]{3,2,1,0:T(4,128)} %bitcast.6, s32[1,256]{1,0:T(1,128)} %bitcast.7, s32[1,256]{1,0:T(1,128)} %bitcast.8, s32[6,256]{1,0:T(8,128)} %neighbours_hbm.1, ...), custom_call_target="tpu_custom_call" | custom-call | tf_op jit(solution)/shard_map/indicator_and_send/pallas_call | solution.py:622
  127.0 1.8 %unpack_slots.1 = (f32[6,125,384]{2,1,0:T(8,128)}, f32[6,125,384]{2,1,0:T(8,128)}, f32[5,5,3,384]{3,2,1,0:T(4,128)}, s32[1,384]{1,0:T(1,128)S(1)}, f32[1,256]{1,0:T(1,128)}) custom-call(f32[16,296,128]{2,1,0:T(8,128)S(1)} %get-tuple-element.12.recv, f32[1,256]{1,0:T(1,128)S(1)} %get-tuple-element.13.share_in), custom_call_target="tpu_custom_call" | custom-call | tf_op jit(solution)/shard_map/unpack_slots/pallas_call | solution.py:680
  128.7 0.6 reduce

commit v2 on v1

--- a/solution.py
+++ b/solution.py
@@ -35,7 +35,8 @@
 BLOCK = COLS * CAP + 8
 PIECES = ((0, 1), (1, 2), (3, 3), (6, 3), (9, 3))
 NEAR = 2
-BEFORE = 4
+FIRST = (3, 8)
+LATER = ((7,), (6,), (5, 4))
 F32 = jnp.float32
 BF16 = jnp.bfloat16
 
@@ -217,6 +218,8 @@
     row_recv,
     sum_send,
     sum_recv,
+    grp_in,
+    dom_in,
 ):
     g = lax.axis_index("grp")
     r = lax.axis_index("dom")
@@ -230,21 +233,33 @@
     def greet(to_g, to_r):
         pl.semaphore_signal(barrier, inc=1, device_id=(to_g, to_r), device_id_type=MESH)
 
-    @pl.loop(1, GRP)
-    def _(k):
-        greet(lax.rem(g + k, GRP), r)
-
-    @pl.loop(1, LEAF)
-    def _(k):
-        greet(g, row * LEAF + lax.rem(lane + k, LEAF))
-
-    @pl.loop(1, ROWS)
-    def _(k):
-        greet(g, lax.rem(row + k, ROWS) * LEAF + lane)
-
+    greet(lax.rem(g + 1, GRP), r)
+    greet(lax.rem(g + GRP - 1, GRP), r)
     greet(g, after)
     greet(g, before)
-    greeted = GRP + LEAF + ROWS - 1
+    greeted = 4
+
+    def tell_grp(n):
+        for to_g in (lax.rem(g + 2**n, GRP), lax.rem(g + GRP - 2**n, GRP)):
+            pl.semaphore_signal(
+                grp_in.at[n], inc=1, device_id=(to_g, r), device_id_type=MESH
+            )
+
+    def tell_dom(n):
+        for to_r in (lax.rem(r + 2**n, DOM), lax.rem(r + DOM - 2**n, DOM)):
+            pl.semaphore_signal(
+                dom_in.at[n], inc=1, device_id=(g, to_r), device_id_type=MESH
+            )
+
+    def told_dom(n):
+        pl.semaphore_wait(dom_in.at[n], 2)
+        if n < 3:
+            tell_dom(n + 1)
+
+    def told_grp(n):
+        pl.semaphore_wait(grp_in.at[n], 2)
+        if n < 2:
+            tell_grp(n + 1)
 
     loads = [
         pltpu.make_async_copy(source, target, load_sem.at[n])
@@ -253,8 +268,8 @@
                 (owner_hbm, owner),
                 (order_hbm, order),
                 (marks_hbm, marks),
+                (factors_hbm, factors),
                 (state_hbm, state),
-                (factors_hbm, factors),
                 (adjoint_hbm, adjoint),
                 (face_u_hbm, face_u),
                 (neighbours_hbm, neighbours),
@@ -267,9 +282,9 @@
     ]
     for load in loads:
         load.start()
-    for load in loads[:5]:
-        load.wait()
-
+
+    top[...] = top_of(MPAD)
+    loads[0].wait()
     to = owner[...]
     hits = jnp.where(lax.broadcasted_iota(jnp.int32, (GRP, ELEM), 0) == to, 1.0, 0.0)
     earlier = jnp.where(
@@ -285,10 +300,11 @@
         lax.broadcasted_iota(jnp.int32, (SLOTS, ELEM), 0) == slot, 1.0, 0.0
     ).astype(BF16)
 
+    for load in loads[1:4]:
+        load.wait()
     level = order[...]
     fresh = jnp.clip(level + marks[...], 1, PMAX)
     low = jnp.minimum(level, fresh)
-    top[...] = top_of(MPAD)
 
     for i in range(P1):
         for j in range(P1):
@@ -350,10 +366,9 @@
     def send_block(k, p=0):
         block_to(k, *blocks[k][p][1:]).start()
 
-    def send_piece(p):
-        for k in partners:
-            if abs(k) <= NEAR:
-                send_block(k, p)
+    def send_piece(p, distance):
+        send_block(distance, p)
+        send_block(-distance, p)
 
     own_block = pltpu.make_async_copy(send.at[g], recv.at[g], self_sem)
 
@@ -366,19 +381,34 @@
         def _(c):
             pack(adjoint, c - NV, fresh, c)
 
+    loads[4].wait()
     for p, (first, count) in enumerate(PIECES):
         if first <= NV < first + count or first == NV:
             loads[5].wait()
         pack_columns(first, count)
         if p == 0:
             pl.semaphore_wait(barrier, greeted)
+            tell_grp(0)
+            tell_dom(0)
         if p == len(PIECES) - 1:
             pack_rest()
-        send_piece(p)
-    for k in partners:
-        if NEAR < abs(k) <= BEFORE:
-            send_block(k)
+        send_piece(p, 1)
+        if p == 0:
+            told_grp(0)
+        send_piece(p, 2)
+    told_grp(1)
+
+    def send_far(distances):
+        for d in distances:
+            send_block(d)
+            if 2 * d != GRP:
+                send_block(-d)
+
+    send_far(FIRST[:1])
+    told_grp(2)
+    send_far(FIRST[1:])
     own_block.start()
+    told_dom(0)
 
     def split_into(target, source, v, most):
         padded_x[0:MODES, :] = jnp.where(top[0:MODES, :] <= most, source[v], 0.0)
@@ -415,11 +445,13 @@
     ]
     for halo in halos:
         halo.start()
+    told_dom(1)
 
     @pl.loop(0, NV)
     def _(v):
         split_into(ps, adjoint, v, level + 1)
 
+    told_dom(2)
     loads[9].wait()
     loads[10].wait()
     near[...] = jnp.zeros(near.shape, F32)
@@ -465,6 +497,7 @@
 
     for halo in halos:
         halo.wait()
+    told_dom(3)
 
     @pl.loop(0, 6)
     def _(f):
@@ -518,9 +551,7 @@
         def _(k):
             one(k).start()
 
-        for k in partners:
-            if abs(k) in then:
-                send_block(k)
+        send_far(then)
 
         @pl.loop(1, count)
         def _(k):
@@ -532,18 +563,18 @@
     part = exchange(
         leaf_sum, lane, LEAF, leaf_send, leaf_recv,
         lambda k: (g, row * LEAF + lax.rem(lane + k, LEAF)),
-        (BEFORE + 1,),
+        LATER[0],
     )
     row_sum[row] = part
     part = exchange(
         row_sum, row, ROWS, row_send, row_recv,
         lambda k: (g, lax.rem(row + k, ROWS) * LEAF + lane),
-        (BEFORE + 2,),
+        LATER[1],
     )
     grp_sum[g] = part
     part = exchange(
         grp_sum, g, GRP, sum_send, sum_recv, lambda k: (lax.rem(g + k, GRP), r),
-        range(BEFORE + 3, GRP),
+        LATER[2],
     )
     mean = part[0:1, 0:1] / (ELEM * GRP * DOM)
     share[...] = eta / (mean + 1e-06)
@@ -672,6 +703,8 @@
             dma((ROWS,)),
             dma((GRP,)),
             dma((GRP,)),
+            pltpu.SemaphoreType.REGULAR((3,)),
+            pltpu.SemaphoreType.REGULAR((4,)),
         ],
         compiler_params=pltpu.CompilerParams(
             collective_id=0, has_side_effects=True, vmem_limit_bytes=32 << 20

time: 129 us -> 127 us (0.984)
  Pallas kernels: 128 us -> 126 us
    pallas_call x1, Pallas kernels: 126 us -> 124 us  [body(): pl.pallas_call(work, name='indicator_and_send', out_shape=(pltpu.VMEM((GR...]
where the time goes in v2:
time: 127 us
  Pallas kernels  126 us (99%)
    pallas_call x1, Pallas kernels, body(): pl.pallas_call(work, name='indicator_and_send', out_shape=(pltpu.VMEM((GR...  124 us

profile of v2, /device:TPU:32, one launch (start us, length us, event | category | flops | bytes accessed | tf_op | source)
XLA Modules:
  0.0 126.8 jit_solution(12790969149600938964)
XLA Ops:
  0.6 123.8 %indicator_and_send.1 = (f32[16,296,128]{2,1,0:T(8,128)S(1)}, f32[1,256]{1,0:T(1,128)S(1)}) custom-call(f32[6,125,256]{2,1,0:T(8,128)} %state_hbm.1, f32[6,125,256]{2,1,0:T(8,128)} %adjoint_hbm.1, f32[5,5,3,256]{3,2,1,0:T(4,128)} %bitcast.6, s32[1,256]{1,0:T(1,128)} %bitcast.7, s32[1,256]{1,0:T(1,128)} %bitcast.8, s32[6,256]{1,0:T(8,128)} %neighbours_hbm.1, ...), custom_call_target="tpu_custom_call" | custom-call | tf_op jit(solution)/shard_map/indicator_and_send/pallas_call | solution.py:653
  124.4 1.8 %unpack_slots.1 = (f32[6,125,384]{2,1,0:T(8,128)}, f32[6,125,384]{2,1,0:T(8,128)}, f32[5,5,3,384]{3,2,1,0:T(4,128)}, s32[1,384]{1,0:T(1,128)S(1)}, f32[1,256]{1,0:T(1,128)}) custom-call(f32[16,296,128]{2,1,0:T(8,128)S(1)} %get-tuple-element.12.recv, f32[1,256]{1,0:T(1,128)S(1)} %get-tuple-element.13.share_in), custom_call_target="tpu_custom_call" | custom-call | tf_op jit(solution)/shard_map/unpack_slots/pallas_call | solution.py:713
  126.2 0.6 reduce

commit v3 on v2

--- a/solution.py
+++ b/solution.py
@@ -624,7 +624,7 @@
             at = (i * P1 + j) * 3
             factors[i, j] = whole[at : at + 3]
     put(factors, moved_factors)
-    order[...] = whole[FROWS - 1 : FROWS].astype(jnp.int32)
+    order[...] = whole[FROWS - 1 : FROWS].astype(jnp.int32).reshape(SLOTS)
     put(order, moved_order)
     for copy in copies:
         copy.wait()
@@ -717,7 +717,7 @@
             jax.ShapeDtypeStruct((NV, MODES, SLOTS), F32),
             jax.ShapeDtypeStruct((NV, MODES, SLOTS), F32),
             jax.ShapeDtypeStruct((P1, P1, 3, SLOTS), F32),
-            jax.ShapeDtypeStruct((1, SLOTS), jnp.int32),
+            jax.ShapeDtypeStruct((SLOTS,), jnp.int32),
             jax.ShapeDtypeStruct((1, ELEM), F32),
         ),
         in_specs=[vmem, vmem],
@@ -726,7 +726,7 @@
             pltpu.VMEM((COLS, MODES, SLOTS), F32),
             pltpu.VMEM((COLS, 8, SLOTS), F32),
             pltpu.VMEM((P1, P1, 3, SLOTS), F32),
-            pltpu.VMEM((1, SLOTS), jnp.int32),
+            pltpu.VMEM((SLOTS,), jnp.int32),
             dma((COLS + 3,)),
         ],
         compiler_params=pltpu.CompilerParams(vmem_limit_bytes=24 << 20),
@@ -736,7 +736,7 @@
         moved_state,
         moved_adjoint,
         moved_factors.transpose(2, 0, 1, 3),
-        moved_order.reshape(SLOTS),
+        moved_order,
     )
 
 

time: 127 us -> 126 us (level)
  no operation moved by 1% of the time
where the time goes in v3:
time: 126 us
  Pallas kernels  126 us (100%)
    pallas_call x1, Pallas kernels, body(): pl.pallas_call(work, name='indicator_and_send', out_shape=(pltpu.VMEM((GR...  124 us

profile of v3, /device:TPU:32, one launch (start us, length us, event | category | flops | bytes accessed | tf_op | source)
XLA Modules:
  0.0 126.2 jit_solution(11240050960053689718)
XLA Ops:
  0.6 123.8 %indicator_and_send.1 = (f32[16,296,128]{2,1,0:T(8,128)S(1)}, f32[1,256]{1,0:T(1,128)S(1)}) custom-call(f32[6,125,256]{2,1,0:T(8,128)} %state_hbm.1, f32[6,125,256]{2,1,0:T(8,128)} %adjoint_hbm.1, f32[5,5,3,256]{3,2,1,0:T(4,128)} %bitcast.6, s32[1,256]{1,0:T(1,128)} %bitcast.7, s32[1,256]{1,0:T(1,128)} %bitcast.8, s32[6,256]{1,0:T(8,128)} %neighbours_hbm.1, ...), custom_call_target="tpu_custom_call" | custom-call | tf_op jit(solution)/shard_map/indicator_and_send/pallas_call | solution.py:653
  124.4 1.8 %unpack_slots.1 = (f32[6,125,384]{2,1,0:T(8,128)}, f32[6,125,384]{2,1,0:T(8,128)}, f32[5,5,3,384]{3,2,1,0:T(4,128)}, s32[384]{0:T(512)}, f32[1,256]{1,0:T(1,128)}) custom-call(f32[16,296,128]{2,1,0:T(8,128)S(1)} %get-tuple-element.12.recv, f32[1,256]{1,0:T(1,128)S(1)} %get-tuple-element.13.share_in), custom_call_target="tpu_custom_call" | custom-call | tf_op jit(solution)/shard_map/unpack_slots/pallas_call | solution.py:713

commit v4 on v3

--- a/solution.py
+++ b/solution.py
@@ -33,7 +33,7 @@
 MESH = pl.DeviceIdType.MESH
 COLS = 2 * NV
 BLOCK = COLS * CAP + 8
-PIECES = ((0, 1), (1, 2), (3, 3), (6, 3), (9, 3))
+PIECES = ((0, 1), (1, 1), (2, 2), (4, 2), (6, 3), (9, 3))
 NEAR = 2
 FIRST = (3, 8)
 LATER = ((7,), (6,), (5, 4))

time: 126 us -> 127 us (level)
  the two profiles are of different devices: /device:TPU:32 before, /device:TPU:35 now
where the time goes in v4:
time: 127 us
  Pallas kernels  126 us (99%)
    pallas_call x1, Pallas kernels, body(): pl.pallas_call(work, name='indicator_and_send', out_shape=(pltpu.VMEM((GR...  124 us

profile of v4, /device:TPU:35, one launch (start us, length us, event | category | flops | bytes accessed | tf_op | source)
XLA Modules:
  0.0 126.8 jit_solution(1599446715005114575)
XLA Ops:
  0.6 124.4 %indicator_and_send.1 = (f32[16,296,128]{2,1,0:T(8,128)S(1)}, f32[1,256]{1,0:T(1,128)S(1)}) custom-call(f32[6,125,256]{2,1,0:T(8,128)} %state_hbm.1, f32[6,125,256]{2,1,0:T(8,128)} %adjoint_hbm.1, f32[5,5,3,256]{3,2,1,0:T(4,128)} %bitcast.6, s32[1,256]{1,0:T(1,128)} %bitcast.7, s32[1,256]{1,0:T(1,128)} %bitcast.8, s32[6,256]{1,0:T(8,128)} %neighbours_hbm.1, ...), custom_call_target="tpu_custom_call" | custom-call | tf_op jit(solution)/shard_map/indicator_and_send/pallas_call | solution.py:653
  125.0 1.8 %unpack_slots.1 = (f32[6,125,384]{2,1,0:T(8,128)}, f32[6,125,384]{2,1,0:T(8,128)}, f32[5,5,3,384]{3,2,1,0:T(4,128)}, s32[384]{0:T(512)}, f32[1,256]{1,0:T(1,128)}) custom-call(f32[16,296,128]{2,1,0:T(8,128)S(1)} %get-tuple-element.12.recv, f32[1,256]{1,0:T(1,128)S(1)} %get-tuple-element.13.share_in), custom_call_target="tpu_custom_call" | custom-call | tf_op jit(solution)/shard_map/unpack_slots/pallas_call | solution.py:713
